TPU v7x, 32 devices: a whole 2x2x4 slice. The times are simulated.
32 devices in a mesh: row: 8 (over y, x, core), col: 4 (over z).
Axes of the slice: x: 2, y: 2, z: 4, core: 2. Of those that a mesh axis runs over, the one named last changes fastest.
Arguments:
- embeddings: bfloat16 [4096, 256], P(('row', 'col')), may hold values from -6 to 6
- cotangent: bfloat16 [4096, 256], P(('row', 'col')), may hold values from -6 to 6
- weight: bfloat16 [256, 256], replicated, may hold values from -0.375 to 0.375
- tiles: bfloat16 [32, 128, 128, 128], P(('row', 'col')), may hold values from -0.078125 to 0.078125
- tile_dst: int32 [32, 128], P(('row', 'col')), may hold values from 0 to 3
- tile_src: int32 [32, 128], P(('row', 'col')), may hold values from 0 to 7
- tile_count: int32 [32], P(('row', 'col')), may hold values from 1 to 128, as said below
Outputs:
- output: bfloat16 [4096, 256], P(('row', 'col'))
- grad_embeddings: bfloat16 [4096, 256], P(('row', 'col'))
- grad_weight: float32 [256, 256], replicated
Inputs may be any that keep to these rules, and one draw needn't show every extreme that they name: `tile_count`: at least one device has exactly 128 live slots.
All inputs are finite; a program needn't handle non-finite values.
Results may differ from a plain program's by a relative error of at most 0.012.
Values may be sent and summed in bfloat16 or wider, within the bound.
A program may use at most 128 MiB of HBM per device.

v0:
```python
import math
import jax
import jax.numpy as jnp
from jax import lax
from jax.sharding import PartitionSpec as P


def shards(embeddings, cotangent, weight, tiles, tile_dst, tile_src, tile_count):
    highest = lax.Precision.HIGHEST
    block_rows = embeddings.shape[0]
    feature_width = embeddings.shape[1]
    row_count = lax.axis_size("row")
    column_count = lax.axis_size("col")
    local_tiles = tiles[0]
    dest_ids = tile_dst[0]
    source_ids = tile_src[0]
    slot_ids = jnp.arange(local_tiles.shape[0], dtype=jnp.int32)
    alive_slots = (slot_ids < tile_count[0]).astype(jnp.float32)
    dest_onehot = (dest_ids[:, None] == jnp.arange(column_count, dtype=jnp.int32)[None, :]).astype(
        jnp.float32
    ) * alive_slots[:, None]
    source_onehot = (source_ids[:, None] == jnp.arange(row_count, dtype=jnp.int32)[None, :]).astype(
        jnp.float32
    ) * alive_slots[:, None]
    gathered = lax.all_gather(embeddings, "row", axis=0, tiled=True).reshape(
        row_count, block_rows, feature_width
    )
    chosen = jnp.take(gathered, source_ids, axis=0)
    products = jnp.einsum("tij,tjd->tid", local_tiles, chosen, preferred_element_type=jnp.float32)
    partial_value = jnp.einsum("tc,tid->cid", dest_onehot, products, precision=highest)
    partial_rounded = partial_value.astype(jnp.bfloat16).reshape(
        column_count * block_rows, feature_width
    )
    summed = lax.psum_scatter(
        partial_rounded.astype(jnp.float32).astype(jnp.bfloat16),
        "col",
        scatter_dimension=0,
        tiled=True,
    ).astype(jnp.float32)
    hidden = summed.astype(jnp.bfloat16)
    output = jnp.dot(hidden, weight, preferred_element_type=jnp.float32).astype(jnp.bfloat16)
    user_count = block_rows * row_count * column_count
    scale_factor = 1.0 / math.sqrt(user_count)
    contract_rows = (((0,), (0,)), ((), ()))
    contract_cols = (((1,), (1,)), ((), ()))
    grad_hidden = lax.dot_general(
        cotangent, weight, contract_cols, preferred_element_type=jnp.float32
    ).astype(jnp.bfloat16)
    grad_group = lax.all_gather(grad_hidden, "col", axis=0, tiled=True)
    weight_term = lax.dot_general(
        summed, cotangent.astype(jnp.float32), contract_rows, precision=highest
    )
    grad_weight = lax.psum(weight_term, ("row", "col")) * scale_factor
    dest_rows = grad_group.reshape(column_count, block_rows, feature_width)
    picked = jnp.take(dest_rows, dest_ids, axis=0)
    back_products = jnp.einsum(
        "tji,tjd->tid", local_tiles, picked, preferred_element_type=jnp.float32
    )
    back_partial = jnp.einsum("tr,tid->rid", source_onehot, back_products, precision=highest)
    back_rounded = lax.optimization_barrier(back_partial.astype(jnp.bfloat16)).astype(jnp.float32)
    back_summed = lax.psum_scatter(
        back_rounded.reshape(row_count * block_rows, feature_width).astype(jnp.bfloat16),
        "row",
        scatter_dimension=0,
        tiled=True,
    )
    return (output, back_summed, grad_weight)


def solution(mesh):
    in_specs = (
        P(("row", "col"), None),
        P(("row", "col"), None),
        P(),
        P(("row", "col"), None, None, None),
        P(("row", "col"), None),
        P(("row", "col"), None),
        P(("row", "col")),
    )
    out_specs = (P(("row", "col"), None), P(("row", "col"), None), P())
    return jax.shard_map(shards, mesh=mesh, in_specs=in_specs, out_specs=out_specs, check_vma=False)
```

profile of v0, /device:TPU:0, one launch (start us, length us, event | category | flops | bytes accessed | tf_op | source)
XLA Modules:
  0.0 260.4 jit_solution(8117860961400061152)
XLA Ops:
  8.0 0.0 copy-start
  8.0 0.0 reduce-scatter.3.cloned.1.call-start
  8.1 0.7 fusion.30
  8.7 0.7 compare_and_fusion.1
  9.4 11.6 %all_gather.6 = bf16[1024,256]{1,0:T(8,128)(2,1)S(1)} all-gather(bf16[128,256]{1,0:T(8,128)(2,1)} %param.7), channel_id=1, replica_groups=mesh['row'=8,'col'=4] {'row'}, dimensions={0}, use_global_device_ids=true | all-gather | bytes 589824 | tf_op jit(solution)/shard_map/all_gather | solution.py:25
  21.0 6.5 %gather_fusion = bf16[128,128,256]{2,1,0:T(8,128)(2,1)} fusion(bf16[8,128,256]{2,1,0:T(8,128)(2,1)S(1)} %bitcast.46, s32[1024]{0:T(1024)S(1)} %pad_clamp_fusion.1), kind=kCustom, calls=%fused_computation | custom fusion | bytes 16777728 | tf_op jit(solution)/shard_map/jit(_take)/gather | solution.py:28
  27.5 13.1 %fusion.6 = f32[128,256,128]{2,1,0:T(8,128)} fusion(bf16[128,128,256]{2,1,0:T(8,128)(2,1)} %gather_fusion, pred[128]{0:T(512)(128)(4,1)S(1)} %compare_and_fusion.1, bf16[1,128,128,128]{3,2,1,0:T(8,128)(2,1)} %param.10), kind=kOutput, calls=%fused_computation.8 | convolution fusion | flops 1077936128 | bytes 29360256 | tf_op jit(solution)/shard_map/tij,tjd->tid/dot_general | solution.py:29
  40.6 0.0 copy-start.3
  40.6 17.7 %copy.12 = f32[128,256,128]{1,0,2:T(8,128)} copy(f32[128,256,128]{2,1,0:T(8,128)} %fusion.6) | data formatting | bytes 33554432 | tf_op jit(solution)/shard_map/tij,tjd->tid/dot_general | solution.py:29
  59.0 0.0 copy-done.3
  59.0 0.0 copy-start.1
  59.0 10.8 %fusion.17 = bf16[4,128,256]{2,0,1:T(4,128)(2,1)S(1)} fusion(f32[128,256,128]{1,0,2:T(8,128)} %copy.12, f32[128]{0:T(128)S(1)} %compare_convert_fusion, s32[128]{0:T(128)S(1)} %bitcast.49), kind=kOutput, calls=%fused_computation.17 | convolution fusion | flops 201458688 | bytes 17040384 | tf_op jit(solution)/shard_map/tc,tid->cid/dot_general | solution.py:30
  69.8 0.7 copy.10
  70.6 0.0 reduce-scatter.3.cloned.1.call-update
  70.6 0.0 all-reduce.2.cloned.1.call-start
  70.7 0.0 copy-done
  70.7 0.0 copy-done.1
  70.7 0.2 convolution_convert_fusion
  70.9 15.5 %all_gather.7 = bf16[512,256]{1,0:T(8,128)(2,1)S(1)} all-gather(bf16[128,256]{1,0:T(8,128)(2,1)S(1)} %convolution_convert_fusion), channel_id=1, replica_groups=mesh['row'=8,'col'=4] {'col'}, dimensions={0}, use_global_device_ids=true | all-gather | bytes 327680 | tf_op jit(solution)/shard_map/all_gather | solution.py:49
  86.4 6.5 %gather_fusion.1 = bf16[128,128,256]{2,1,0:T(8,128)(2,1)} fusion(bf16[4,128,256]{2,1,0:T(8,128)(2,1)S(1)} %bitcast.45, s32[1024]{0:T(1024)S(1)} %pad_clamp_fusion), kind=kCustom, calls=%fused_computation.1 | custom fusion | bytes 16777728 | tf_op jit(solution)/shard_map/jit(_take)/gather | solution.py:55
  92.9 12.8 %fusion.4 = f32[128,256,128]{2,1,0:T(8,128)} fusion(bf16[128,128,256]{2,1,0:T(8,128)(2,1)} %gather_fusion.1, pred[128]{0:T(512)(128)(4,1)S(1)} %compare_and_fusion, bf16[1,128,128,128]{3,2,1,0:T(8,128)(2,1)} %param.10), kind=kOutput, calls=%fused_computation.6 | convolution fusion | flops 1077936128 | bytes 29360256 | tf_op jit(solution)/shard_map/tji,tjd->tid/dot_general | solution.py:56
  105.7 0.0 copy-start.4
  105.7 17.7 %copy.13 = f32[128,256,128]{1,0,2:T(8,128)} copy(f32[128,256,128]{2,1,0:T(8,128)} %fusion.4) | data formatting | bytes 33554432 | tf_op jit(solution)/shard_map/tji,tjd->tid/dot_general | solution.py:56
  123.4 0.0 reduce-scatter.3.cloned.1.call-done
  123.4 1.7 fusion.36
  125.1 0.0 all-reduce.2.cloned.1.call-update
  125.2 0.0 reduce-scatter.5.cloned.1.call-start
  125.2 0.0 copy-done.4
  125.2 0.0 copy-start.2
  125.2 10.8 %fusion.14 = bf16[8,128,256]{2,0,1:T(8,128)(2,1)S(1)} fusion(f32[128,256,128]{1,0,2:T(8,128)} %copy.13, f32[128]{0:T(128)S(1)} %compare_convert_fusion, s32[128]{0:T(128)S(1)} %bitcast.50), kind=kOutput, calls=%fused_computation.16 | convolution fusion | flops 402917376 | bytes 17302528 | tf_op jit(solution)/shard_map/tr,tid->rid/dot_general | solution.py:59
  136.1 0.9 copy.11
  137.0 0.0 reduce-scatter.5.cloned.1.call-update
  137.0 0.0 copy-done.2
  137.0 0.8 convolution_convert_fusion.1
  137.8 113.4 %all-reduce.2.cloned.1.call-done = f32[256,256]{1,0:T(8,128)} async-done(((f32[256,256]{1,0:T(8,128)}), f32[256,256]{1,0:T(8,128)}) %all-reduce.2.cloned.1.call-update) | async-done | bytes 262160 | tf_op jit(solution)/shard_map/psum | solution.py:53
  251.3 1.7 broadcast_multiply_fusion
  252.9 0.0 reduce-scatter.5.cloned.1.call-done
  (5 shorter events, 0.0 us)
Async XLA Ops:
  8.0 62.7 %copy-start = (bf16[256,256]{1,0:T(8,128)(2,1)S(1)}, bf16[256,256]{1,0:T(8,128)(2,1)}, u32[]{:S(2)}) copy-start(bf16[256,256]{1,0:T(8,128)(2,1)} %param.9) | copy-start | bytes 393220
  8.0 115.4 %reduce-scatter.3.cloned.1.call-start = ((), (), s32[]{:S(2)}) async-start(), calls=%async_computation.2 | async-start | bytes 327680 | tf_op jit(solution)/shard_map/reduce_scatter | solution.py:34
  40.6 18.4 %copy-start.3 = (s32[1,128]{1,0:T(1,128)S(1)}, s32[1,128]{1,0:T(1,128)}, u32[]{:S(2)}) copy-start(s32[1,128]{1,0:T(1,128)} %param.11) | copy-start | bytes 1540
  59.0 11.7 %copy-start.1 = (bf16[128,256]{1,0:T(8,128)(2,1)S(1)}, bf16[128,256]{1,0:T(8,128)(2,1)}, u32[]{:S(2)}) copy-start(bf16[128,256]{1,0:T(8,128)(2,1)} %param.8) | copy-start | bytes 196612
  70.6 180.7 %all-reduce.2.cloned.1.call-start = ((), (), s32[]{:S(2)}) async-start(), calls=%async_computation.4 | async-start | bytes 524288 | tf_op jit(solution)/shard_map/psum | solution.py:53
  105.7 19.5 %copy-start.4 = (s32[1,128]{1,0:T(1,128)S(1)}, s32[1,128]{1,0:T(1,128)}, u32[]{:S(2)}) copy-start(s32[1,128]{1,0:T(1,128)} %param.12) | copy-start | bytes 1540
  125.2 127.8 %reduce-scatter.5.cloned.1.call-start = ((), (), s32[]{:S(2)}) async-start(), calls=%async_computation.3 | async-start | bytes 589824 | tf_op jit(solution)/shard_map/reduce_scatter | solution.py:61
  125.2 11.8 %copy-start.2 = (bf16[128,256]{1,0:T(8,128)(2,1)S(1)}, bf16[128,256]{1,0:T(8,128)(2,1)}, u32[]{:S(2)}) copy-start(bf16[128,256]{1,0:T(8,128)(2,1)} %reduce-scatter.3.cloned.1.call-done) | copy-start | bytes 196612
Sparse Core Ops, SparseCore 0:
  70.7 20.6 reduce-scatter.2
  125.3 125.9 all-reduce.1
Sparse Core Ops, SparseCore 1:
  137.1 34.8 reduce-scatter.4
where the time goes:
time: 261 us; the launch traced here: 260 us
  waiting for transfers between devices  113 us (43%)
  matrix products  50.3 us (19%)
  local copies, waits for them, and re-layouts  50 us (19%)
  blocking collectives  27.1 us (10%)
  between operations  16.3 us (6%)
  other arithmetic  3.05 us (1%)
    psum x1, waiting for transfers between devices, shards(): grad_weight = lax.psum(weight_term, ('row', 'col')) * scale_factor  113 us
    dot_general x1, local copies, waits for them, and re-layouts, shards(): jnp.einsum('tij,tjd->tid', local_tiles, chosen, preferred_element_type=jn...  17.7 us
    dot_general x1, local copies, waits for them, and re-layouts, shards(): jnp.einsum('tji,tjd->tid', local_tiles, picked, preferred_element_type=jn...  17.7 us
    all_gather x1, blocking collectives, shards(): grad_group = lax.all_gather(grad_hidden, 'col', axis=0, tiled=True)  15.5 us
    dot_general x1, matrix products, shards(): jnp.einsum('tij,tjd->tid', local_tiles, chosen, preferred_element_type=jn...  13.1 us
    dot_general x1, matrix products, shards(): jnp.einsum('tji,tjd->tid', local_tiles, picked, preferred_element_type=jn...  12.8 us
    all_gather x1, blocking collectives, shards(): lax.all_gather(embeddings, 'row', axis=0, tiled=True)  11.6 us
    dot_general x1, matrix products, shards(): jnp.einsum('tc,tid->cid', dest_onehot, products, precision=highest)  10.8 us
  transfers between devices with their start and end apart: 3, of which 1 were waited for; matrix products, arithmetic and copies ran while one was open for 20% of the time, Pallas kernels for 0%

commit v1 on v0

--- a/solution.py
+++ b/solution.py
@@ -1,8 +1,16 @@
+import functools
 import math
 import jax
 import jax.numpy as jnp
 from jax import lax
 from jax.sharding import PartitionSpec as P
+
+
+def form_trees_in(block_here, group_axis):
+    return lax.all_gather(block_here, group_axis).sum(axis=0)
+
+
+wrap_sectors = functools.partial(form_trees_in, group_axis=("row", "col"))
 
 
 def shards(embeddings, cotangent, weight, tiles, tile_dst, tile_src, tile_count):
@@ -50,7 +58,7 @@
     weight_term = lax.dot_general(
         summed, cotangent.astype(jnp.float32), contract_rows, precision=highest
     )
-    grad_weight = lax.psum(weight_term, ("row", "col")) * scale_factor
+    grad_weight = wrap_sectors(weight_term) * scale_factor
     dest_rows = grad_group.reshape(column_count, block_rows, feature_width)
     picked = jnp.take(dest_rows, dest_ids, axis=0)
     back_products = jnp.einsum(

time: 261 us -> 199 us (0.76)
  waiting for transfers between devices: 113 us -> 48.2 us
  other arithmetic: 3.05 us -> 6.03 us
    psum x1 -> x0, waiting for transfers between devices: 113 us -> none  [shards(): grad_weight = lax.psum(weight_term, ('row', 'col')) * scale_factor]
    reduce_scatter x1, waiting for transfers between devices: 0.01 us -> 20.1 us  [shards(): lax.psum_scatter(partial_rounded.astype(jnp.float32).astype(jnp.bfloat16)...]
    reduce_scatter x1, waiting for transfers between devices: 0.01 us -> 15.2 us  [shards(): lax.psum_scatter(back_rounded.reshape(row_count * block_rows, feature_wid...]
    all_gather x0 -> x1, waiting for transfers between devices: none -> 12.9 us  [form_trees_in(): return lax.all_gather(block_here, group_axis).sum(axis=0)]
    reduce_sum x0 -> x1, other arithmetic: none -> 3.93 us  [form_trees_in(): return lax.all_gather(block_here, group_axis).sum(axis=0)]
  transfers between devices with their start and end apart: 3 -> 3, of which waited for: 1 -> 3; matrix products, arithmetic and copies ran while one was open for 20% -> 28% of each run, Pallas kernels for 0% -> 0%
where the time goes in v1:
time: 199 us; the launch traced here: 198 us
  matrix products  50.4 us (25%)
  local copies, waits for them, and re-layouts  50.2 us (25%)
  waiting for transfers between devices  48.2 us (24%)
  blocking collectives  26.7 us (13%)
  between operations  16.2 us (8%)
  other arithmetic  6.03 us (3%)
    reduce_scatter x1, waiting for transfers between devices, shards(): lax.psum_scatter(partial_rounded.astype(jnp.float32).astype(jnp.bfloat16)...  20.1 us
    dot_general x1, local copies, waits for them, and re-layouts, shards(): jnp.einsum('tji,tjd->tid', local_tiles, picked, preferred_element_type=jn...  17.9 us
    dot_general x1, local copies, waits for them, and re-layouts, shards(): jnp.einsum('tij,tjd->tid', local_tiles, chosen, preferred_element_type=jn...  17.7 us
    reduce_scatter x1, waiting for transfers between devices, shards(): lax.psum_scatter(back_rounded.reshape(row_count * block_rows, feature_wid...  15.2 us
    all_gather x1, blocking collectives, shards(): grad_group = lax.all_gather(grad_hidden, 'col', axis=0, tiled=True)  15.2 us
    dot_general x1, matrix products, shards(): jnp.einsum('tij,tjd->tid', local_tiles, chosen, preferred_element_type=jn...  13.1 us
    all_gather x1, waiting for transfers between devices, form_trees_in(): return lax.all_gather(block_here, group_axis).sum(axis=0)  12.9 us
    dot_general x1, matrix products, shards(): jnp.einsum('tji,tjd->tid', local_tiles, picked, preferred_element_type=jn...  12.8 us
  transfers between devices with their start and end apart: 3, of which 3 were waited for; matrix products, arithmetic and copies ran while one was open for 28% of the time, Pallas kernels for 0%

profile of v1, /device:TPU:0, one launch (start us, length us, event | category | flops | bytes accessed | tf_op | source)
XLA Modules:
  0.0 197.9 jit_solution(13044373291319878355)
XLA Ops:
  8.0 0.0 copy-start
  8.0 0.0 reduce-scatter.3.cloned.1.call-start
  8.1 0.7 fusion.30
  8.7 0.7 compare_and_fusion.1
  9.4 11.6 %all_gather.12 = bf16[1024,256]{1,0:T(8,128)(2,1)S(1)} all-gather(bf16[128,256]{1,0:T(8,128)(2,1)} %param.7), channel_id=1, replica_groups=mesh['row'=8,'col'=4] {'row'}, dimensions={0}, use_global_device_ids=true | all-gather | bytes 589824 | tf_op jit(solution)/shard_map/all_gather | solution.py:33
  21.0 6.5 %gather_fusion = bf16[128,128,256]{2,1,0:T(8,128)(2,1)} fusion(bf16[8,128,256]{2,1,0:T(8,128)(2,1)S(1)} %bitcast.47, s32[1024]{0:T(1024)S(1)} %pad_clamp_fusion.1), kind=kCustom, calls=%fused_computation | custom fusion | bytes 16777728 | tf_op jit(solution)/shard_map/jit(_take)/gather | solution.py:36
  27.5 13.1 %fusion.6 = f32[128,256,128]{2,1,0:T(8,128)} fusion(bf16[128,128,256]{2,1,0:T(8,128)(2,1)} %gather_fusion, pred[128]{0:T(512)(128)(4,1)S(1)} %compare_and_fusion.1, bf16[1,128,128,128]{3,2,1,0:T(8,128)(2,1)} %param.10), kind=kOutput, calls=%fused_computation.8 | convolution fusion | flops 1077936128 | bytes 29360256 | tf_op jit(solution)/shard_map/tij,tjd->tid/dot_general | solution.py:37
  40.6 0.0 copy-start.3
  40.6 17.7 %copy.12 = f32[128,256,128]{1,0,2:T(8,128)} copy(f32[128,256,128]{2,1,0:T(8,128)} %fusion.6) | data formatting | bytes 33554432 | tf_op jit(solution)/shard_map/tij,tjd->tid/dot_general | solution.py:37
  59.0 0.0 copy-done.3
  59.0 0.0 copy-start.1
  59.0 10.8 %fusion.17 = bf16[4,128,256]{2,0,1:T(4,128)(2,1)S(1)} fusion(f32[128,256,128]{1,0,2:T(8,128)} %copy.12, f32[128]{0:T(128)S(1)} %compare_convert_fusion, s32[128]{0:T(128)S(1)} %bitcast.51), kind=kOutput, calls=%fused_computation.17 | convolution fusion | flops 201458688 | bytes 17040384 | tf_op jit(solution)/shard_map/tc,tid->cid/dot_general | solution.py:38
  69.8 0.7 copy.10
  70.6 0.0 reduce-scatter.3.cloned.1.call-update
  70.6 0.0 all-gather.3.cloned.1.call-start
  70.7 20.1 %reduce-scatter.3.cloned.1.call-done = bf16[128,256]{1,0:T(8,128)(2,1)} async-done(((bf16[512,256]{1,0:T(8,128)(2,1)}), bf16[128,256]{1,0:T(8,128)(2,1)}) %reduce-scatter.3.cloned.1.call-update) | async-done | bytes 65552 | tf_op jit(solution)/shard_map/reduce_scatter | solution.py:42
  90.7 0.0 copy-done.1
  90.7 1.7 fusion.36
  92.5 0.0 all-gather.3.cloned.1.call-update
  92.5 0.0 reduce-scatter.5.cloned.1.call-start
  92.5 0.0 copy-done
  92.5 0.2 convolution_convert_fusion
  92.7 15.2 %all_gather.13 = bf16[512,256]{1,0:T(8,128)(2,1)S(1)} all-gather(bf16[128,256]{1,0:T(8,128)(2,1)S(1)} %convolution_convert_fusion), channel_id=1, replica_groups=mesh['row'=8,'col'=4] {'col'}, dimensions={0}, use_global_device_ids=true | all-gather | bytes 327680 | tf_op jit(solution)/shard_map/all_gather | solution.py:57
  107.9 6.5 %gather_fusion.1 = bf16[128,128,256]{2,1,0:T(8,128)(2,1)} fusion(bf16[4,128,256]{2,1,0:T(8,128)(2,1)S(1)} %bitcast.46, s32[1024]{0:T(1024)S(1)} %pad_clamp_fusion), kind=kCustom, calls=%fused_computation.1 | custom fusion | bytes 16777728 | tf_op jit(solution)/shard_map/jit(_take)/gather | solution.py:63
  114.4 12.8 %fusion.4 = f32[128,256,128]{2,1,0:T(8,128)} fusion(bf16[128,128,256]{2,1,0:T(8,128)(2,1)} %gather_fusion.1, pred[128]{0:T(512)(128)(4,1)S(1)} %compare_and_fusion, bf16[1,128,128,128]{3,2,1,0:T(8,128)(2,1)} %param.10), kind=kOutput, calls=%fused_computation.6 | convolution fusion | flops 1077936128 | bytes 29360256 | tf_op jit(solution)/shard_map/tji,tjd->tid/dot_general | solution.py:64
  127.2 0.0 copy-start.4
  127.2 17.9 %copy.13 = f32[128,256,128]{1,0,2:T(8,128)} copy(f32[128,256,128]{2,1,0:T(8,128)} %fusion.4) | data formatting | bytes 33554432 | tf_op jit(solution)/shard_map/tji,tjd->tid/dot_general | solution.py:64
  145.1 0.0 copy-done.4
  145.1 0.0 copy-start.2
  145.1 10.9 %fusion.14 = bf16[8,128,256]{2,0,1:T(8,128)(2,1)S(1)} fusion(f32[128,256,128]{1,0,2:T(8,128)} %copy.13, f32[128]{0:T(128)S(1)} %compare_convert_fusion, s32[128]{0:T(128)S(1)} %bitcast.52), kind=kOutput, calls=%fused_computation.16 | convolution fusion | flops 402917376 | bytes 17302528 | tf_op jit(solution)/shard_map/tr,tid->rid/dot_general | solution.py:67
  156.0 0.9 copy.11
  156.9 0.0 reduce-scatter.5.cloned.1.call-update
  156.9 0.0 copy-done.2
  156.9 0.8 convolution_convert_fusion.1
  157.7 12.9 %all-gather.3.cloned.1.call-done = f32[8192,256]{1,0:T(8,128)} async-done(((f32[256,256]{1,0:T(8,128)}), f32[8192,256]{1,0:T(8,128)}) %all-gather.3.cloned.1.call-update) | async-done | bytes 8388624 | tf_op jit(solution)/shard_map/all_gather | solution.py:10
  170.6 3.9 %reduce_sum.9 = f32[256,256]{1,0:T(8,128)S(1)} reduce(f32[32,256,256]{2,1,0:T(8,128)} %bitcast.48, f32[]{:T(128)} %constant.28.clone.1), dimensions={0}, to_apply=%region_2.3 | reduce | flops 2031616 | bytes 8650756 | tf_op jit(solution)/shard_map/reduce_sum | solution.py:10
  174.6 0.7 broadcast_multiply_fusion
  175.3 15.2 %reduce-scatter.5.cloned.1.call-done = bf16[128,256]{1,0:T(8,128)(2,1)} async-done(((bf16[1024,256]{1,0:T(8,128)(2,1)}), bf16[128,256]{1,0:T(8,128)(2,1)}) %reduce-scatter.5.cloned.1.call-update) | async-done | bytes 65552 | tf_op jit(solution)/shard_map/reduce_scatter | solution.py:69
  (5 shorter events, 0.0 us)
Async XLA Ops:
  8.0 84.5 %copy-start = (bf16[256,256]{1,0:T(8,128)(2,1)S(1)}, bf16[256,256]{1,0:T(8,128)(2,1)}, u32[]{:S(2)}) copy-start(bf16[256,256]{1,0:T(8,128)(2,1)} %param.9) | copy-start | bytes 393220
  8.0 82.7 %reduce-scatter.3.cloned.1.call-start = ((), (), s32[]{:S(2)}) async-start(), calls=%async_computation.2 | async-start | bytes 327680 | tf_op jit(solution)/shard_map/reduce_scatter | solution.py:42
  40.6 18.4 %copy-start.3 = (s32[1,128]{1,0:T(1,128)S(1)}, s32[1,128]{1,0:T(1,128)}, u32[]{:S(2)}) copy-start(s32[1,128]{1,0:T(1,128)} %param.11) | copy-start | bytes 1540
  59.0 31.7 %copy-start.1 = (bf16[128,256]{1,0:T(8,128)(2,1)S(1)}, bf16[128,256]{1,0:T(8,128)(2,1)}, u32[]{:S(2)}) copy-start(bf16[128,256]{1,0:T(8,128)(2,1)} %param.8) | copy-start | bytes 196612
  70.6 100.0 %all-gather.3.cloned.1.call-start = ((), (), s32[]{:S(2)}) async-start(), calls=%async_computation.4 | async-start | bytes 8650752 | tf_op jit(solution)/shard_map/all_gather | solution.py:10
  92.5 98.0 %reduce-scatter.5.cloned.1.call-start = ((), (), s32[]{:S(2)}) async-start(), calls=%async_computation.3 | async-start | bytes 589824 | tf_op jit(solution)/shard_map/reduce_scatter | solution.py:69
  127.2 17.9 %copy-start.4 = (s32[1,128]{1,0:T(1,128)S(1)}, s32[1,128]{1,0:T(1,128)}, u32[]{:S(2)}) copy-start(s32[1,128]{1,0:T(1,128)} %param.12) | copy-start | bytes 1540
  145.1 11.8 %copy-start.2 = (bf16[128,256]{1,0:T(8,128)(2,1)S(1)}, bf16[128,256]{1,0:T(8,128)(2,1)}, u32[]{:S(2)}) copy-start(bf16[128,256]{1,0:T(8,128)(2,1)} %reduce-scatter.3.cloned.1.call-done) | copy-start | bytes 196612
Sparse Core Ops, SparseCore 0:
  70.7 19.9 reduce-scatter.2
  94.2 76.3 all-gather.2
Sparse Core Ops, SparseCore 1:
  157.0 33.4 reduce-scatter.4
